TPU v7x, 32 devices: a whole 2x2x4 slice. The times are simulated.
32 devices in a mesh: dp: 4 (over y, x), tensor: 8 (over z, core).
Axes of the slice: x: 2, y: 2, z: 4, core: 2. Of those that a mesh axis runs over, the one named last changes fastest.
Arguments:
- tokens: bfloat16 [8, 1024, 2048], P('dp', 'tensor'), may hold values from -6 to 6
- cotangent: bfloat16 [8, 1024, 2048], P('dp', 'tensor'), may hold values from -6 to 6
- lengths: int32 [8], P('dp'), may hold values from 256 to 1024, as said below
- ln1_gain: float32 [2048], replicated, may hold values from 0.25 to 1.75
- ln1_shift: float32 [2048], replicated, may hold values from -1.5 to 1.5
- qkv_weight: bfloat16 [3, 2048, 2048], P(None, None, 'tensor'), may hold values from -0.125 to 0.125
- qkv_bias: float32 [2, 2048], P(None, 'tensor'), may hold values from -2.5 to 2.5
- out_weight: bfloat16 [2048, 2048], P('tensor'), may hold values from -1 to 1
- out_bias: float32 [2048], replicated, may hold values from -1.5 to 1.5
- ln2_gain: float32 [2048], replicated, may hold values from 0.25 to 1.75
- ln2_shift: float32 [2048], replicated, may hold values from -1.5 to 1.5
- up_weight: bfloat16 [2048, 8192], P(None, 'tensor'), may hold values from -0.125 to 0.125
- up_bias: float32 [8192], P('tensor'), may hold values from -2.5 to 2.5
- down_weight: bfloat16 [8192, 2048], P('tensor'), may hold values from -0.0625 to 0.0625
- down_bias: float32 [2048], replicated, may hold values from -1.5 to 1.5
Outputs:
- output: bfloat16 [8, 1024, 2048], P('dp', 'tensor')
- input_grad: float32 [8, 1024, 2048], P('dp', 'tensor')
- ln1_gain_grad: float32 [2048], replicated
- ln1_shift_grad: float32 [2048], replicated
- qkv_weight_grad: float32 [3, 2048, 2048], P(None, None, 'tensor')
- qkv_bias_grad: float32 [2, 2048], P(None, 'tensor')
- out_weight_grad: float32 [2048, 2048], P('tensor')
- out_bias_grad: float32 [2048], replicated
- ln2_gain_grad: float32 [2048], replicated
- ln2_shift_grad: float32 [2048], replicated
- up_weight_grad: float32 [2048, 8192], P(None, 'tensor')
- up_bias_grad: float32 [8192], P('tensor')
- down_weight_grad: float32 [8192, 2048], P('tensor')
- down_bias_grad: float32 [2048], replicated
Inputs may be any that keep to these rules, and one draw needn't show every extreme that they name: A sequence's valid tokens are its first lengths[s] slots; some sequence has exactly 1024 and some exactly 256.
All inputs are finite; a program needn't handle non-finite values.
Results may differ from a plain program's by a relative error of at most 0.018.
Values may be sent and summed in bfloat16 or wider, within the bound.
A program may use at most 256 MiB of HBM per device.

v0:
```python
import jax
import jax.numpy as jnp
from jax import lax
from jax.sharding import PartitionSpec as P

HD = 128
norm_epsilon = 1e-05
block_rows = 512


def layer_norm(values, norm_gain, norm_shift):
    centre = values - jnp.mean(values, axis=-1, keepdims=True)
    spread = jnp.mean(centre * centre, axis=-1, keepdims=True)
    return centre * lax.rsqrt(spread + norm_epsilon) * norm_gain + norm_shift


def gelu_exact(values):
    return jax.nn.gelu(values, approximate=False)


def flat_product(left_rows, right_rows):
    flat = left_rows.reshape(-1, left_rows.shape[-1])
    result = jnp.dot(flat, right_rows, preferred_element_type=jnp.float32)
    return result.reshape(left_rows.shape[:-1] + (right_rows.shape[-1],))


def product_back(left_rows, right_rows):
    flat = left_rows.reshape(-1, left_rows.shape[-1])
    result = lax.dot_general(
        flat, right_rows, (((1,), (1,)), ((), ())), preferred_element_type=jnp.float32
    )
    return result.reshape(left_rows.shape[:-1] + (right_rows.shape[0],))


def rows_product(left_rows, right_rows):
    left_flat = left_rows.reshape(-1, left_rows.shape[-1])
    right_flat = right_rows.reshape(-1, right_rows.shape[-1])
    return lax.dot_general(
        left_flat, right_flat, (((0,), (0,)), ((), ())), preferred_element_type=jnp.float32
    )


def allowed_mask(first_row, row_count, slot_count, length):
    row_ids = first_row + lax.broadcasted_iota(jnp.int32, (row_count, slot_count), 0)
    col_ids = lax.broadcasted_iota(jnp.int32, (row_count, slot_count), 1)
    return (col_ids <= row_ids) & (col_ids < length)


def block_scores(query_block, key_rows, first_row, length):
    scores = jnp.einsum("qhd,khd->hqk", query_block, key_rows, preferred_element_type=jnp.float32)
    allowed = allowed_mask(first_row, query_block.shape[0], key_rows.shape[0], length)
    return jnp.where(allowed[None], scores, -1e30)


def attend_forward(query_rows, key_rows, value_rows, length):
    slot_count = query_rows.shape[0]
    step_rows = min(block_rows, slot_count)
    outputs = []
    totals = []
    for block_index in range(slot_count // step_rows):
        first_row = block_index * step_rows
        query_block = query_rows[first_row : first_row + step_rows]
        scores = block_scores(query_block, key_rows, first_row, length)
        row_peak = jnp.max(scores, axis=-1, keepdims=True)
        log_total = row_peak + jnp.log(jnp.sum(jnp.exp(scores - row_peak), axis=-1, keepdims=True))
        weights = jnp.exp(scores - log_total).astype(jnp.bfloat16)
        outputs.append(
            jnp.einsum("hqk,khd->qhd", weights, value_rows, preferred_element_type=jnp.float32)
        )
        totals.append(log_total)
    return (jnp.concatenate(outputs, axis=0), jnp.concatenate(totals, axis=1))


def attend_backward(query_rows, key_rows, value_rows, grad_rows, log_totals, length):
    slot_count = query_rows.shape[0]
    step_rows = min(block_rows, slot_count)
    grad_keys = jnp.zeros(key_rows.shape, jnp.float32)
    grad_values = jnp.zeros(value_rows.shape, jnp.float32)
    grad_queries = []
    for block_index in range(slot_count // step_rows):
        first_row = block_index * step_rows
        query_block = query_rows[first_row : first_row + step_rows]
        grad_block = grad_rows[first_row : first_row + step_rows]
        scores = block_scores(query_block, key_rows, first_row, length)
        probs = jnp.exp(scores - log_totals[:, first_row : first_row + step_rows])
        grad_probs = jnp.einsum(
            "qhd,khd->hqk", grad_block, value_rows, preferred_element_type=jnp.float32
        )
        centre = jnp.sum(probs * grad_probs, axis=-1, keepdims=True)
        grad_scores = (probs * (grad_probs - centre)).astype(jnp.bfloat16)
        grad_queries.append(
            jnp.einsum("hqk,khd->qhd", grad_scores, key_rows, preferred_element_type=jnp.float32)
        )
        grad_keys = grad_keys + jnp.einsum(
            "hqk,qhd->khd", grad_scores, query_block, preferred_element_type=jnp.float32
        )
        grad_values = grad_values + jnp.einsum(
            "hqk,qhd->khd",
            probs.astype(jnp.bfloat16),
            grad_block,
            preferred_element_type=jnp.float32,
        )
    return (jnp.concatenate(grad_queries, axis=0), grad_keys, grad_values)


def body(
    tokens,
    cotangent,
    lengths,
    ln1_gain,
    ln1_shift,
    qkv_weight,
    qkv_bias,
    out_weight,
    out_bias,
    ln2_gain,
    ln2_shift,
    up_weight,
    up_bias,
    down_weight,
    down_bias,
):
    seq_count, local_rows, model_width = tokens.shape
    part_width = qkv_weight.shape[2]
    head_count = part_width // HD
    score_scale = HD ** (-0.5)
    inputs = tokens.astype(jnp.float32)
    normed_one = layer_norm(inputs, ln1_gain, ln1_shift).astype(jnp.bfloat16)
    gathered_one = lax.all_gather(normed_one, "tensor", axis=1, tiled=True)
    slot_count = gathered_one.shape[1]
    head_shape = (seq_count, slot_count, head_count, HD)
    query_rows = (
        ((flat_product(gathered_one, qkv_weight[0]) + qkv_bias[0]) * score_scale)
        .astype(jnp.bfloat16)
        .reshape(head_shape)
    )
    key_rows = flat_product(gathered_one, qkv_weight[1]).astype(jnp.bfloat16).reshape(head_shape)
    value_rows = (
        (flat_product(gathered_one, qkv_weight[2]) + qkv_bias[1])
        .astype(jnp.bfloat16)
        .reshape(head_shape)
    )
    attended, log_totals = lax.map(
        lambda item: attend_forward(item[0], item[1], item[2], item[3]),
        (query_rows, key_rows, value_rows, lengths),
    )
    mixed_heads = attended.reshape(seq_count, slot_count, part_width).astype(jnp.bfloat16)
    attn_local = lax.psum_scatter(
        flat_product(mixed_heads, out_weight).astype(jnp.bfloat16),
        "tensor",
        scatter_dimension=1,
        tiled=True,
    ).astype(jnp.float32)
    hidden_state = inputs + attn_local + out_bias
    normed_two = layer_norm(hidden_state, ln2_gain, ln2_shift).astype(jnp.bfloat16)
    gathered_two = lax.all_gather(normed_two, "tensor", axis=1, tiled=True)
    pre_act = flat_product(gathered_two, up_weight) + up_bias
    activated = gelu_exact(pre_act).astype(jnp.bfloat16)
    mlp_local = lax.psum_scatter(
        flat_product(activated, down_weight).astype(jnp.bfloat16),
        "tensor",
        scatter_dimension=1,
        tiled=True,
    ).astype(jnp.float32)
    output = (hidden_state + mlp_local + down_bias).astype(jnp.bfloat16)
    slot_ids = lax.axis_index("tensor") * local_rows + lax.broadcasted_iota(
        jnp.int32, (seq_count, local_rows), 1
    )
    valid_rows = (slot_ids < lengths[:, None]).astype(jnp.float32)
    grad_out = cotangent.astype(jnp.float32) * valid_rows[:, :, None]
    down_bias_grad = jnp.sum(grad_out, axis=(0, 1))
    grad_mlp = lax.all_gather(grad_out.astype(jnp.bfloat16), "tensor", axis=1, tiled=True)
    down_weight_grad = rows_product(activated, grad_mlp)
    grad_act = product_back(grad_mlp, down_weight)
    unused_act, gelu_back = jax.vjp(gelu_exact, pre_act)
    grad_pre = gelu_back(grad_act)[0].astype(jnp.bfloat16)
    up_bias_grad = jnp.sum(grad_pre.astype(jnp.float32), axis=(0, 1))
    up_weight_grad = rows_product(gathered_two, grad_pre)
    norm_two_grad = lax.psum_scatter(
        product_back(grad_pre, up_weight), "tensor", scatter_dimension=1, tiled=True
    )
    unused_two, norm_two_back = jax.vjp(layer_norm, hidden_state, ln2_gain, ln2_shift)
    hidden_ln_grad, ln2_gain_grad, ln2_shift_grad = norm_two_back(norm_two_grad)
    hidden_grad = grad_out + hidden_ln_grad
    out_bias_grad = jnp.sum(hidden_grad, axis=(0, 1))
    grad_attn = lax.all_gather(hidden_grad.astype(jnp.bfloat16), "tensor", axis=1, tiled=True)
    out_weight_grad = rows_product(mixed_heads, grad_attn)
    grad_heads = product_back(grad_attn, out_weight).astype(jnp.bfloat16).reshape(head_shape)
    grad_query, grad_key, grad_value = lax.map(
        lambda item: attend_backward(item[0], item[1], item[2], item[3], item[4], item[5]),
        (query_rows, key_rows, value_rows, grad_heads, log_totals, lengths),
    )
    flat_shape = (seq_count, slot_count, part_width)
    grad_query = grad_query.reshape(flat_shape).astype(jnp.bfloat16)
    grad_key = grad_key.reshape(flat_shape).astype(jnp.bfloat16)
    grad_value = grad_value.reshape(flat_shape).astype(jnp.bfloat16)
    qkv_weight_grad = jnp.stack(
        [
            score_scale * rows_product(gathered_one, grad_query),
            rows_product(gathered_one, grad_key),
            rows_product(gathered_one, grad_value),
        ]
    )
    qkv_bias_grad = jnp.stack(
        [
            score_scale * jnp.sum(grad_query.astype(jnp.float32), axis=(0, 1)),
            jnp.sum(grad_value.astype(jnp.float32), axis=(0, 1)),
        ]
    )
    norm_one_part = (
        score_scale * product_back(grad_query, qkv_weight[0])
        + product_back(grad_key, qkv_weight[1])
        + product_back(grad_value, qkv_weight[2])
    )
    norm_one_grad = lax.psum_scatter(norm_one_part, "tensor", scatter_dimension=1, tiled=True)
    unused_one, norm_one_back = jax.vjp(layer_norm, inputs, ln1_gain, ln1_shift)
    input_ln_grad, ln1_gain_grad, ln1_shift_grad = norm_one_back(norm_one_grad)
    input_grad = hidden_grad + input_ln_grad
    (
        qkv_weight_grad,
        qkv_bias_grad,
        out_weight_grad,
        up_weight_grad,
        up_bias_grad,
        down_weight_grad,
    ) = lax.psum(
        (
            qkv_weight_grad,
            qkv_bias_grad,
            out_weight_grad,
            up_weight_grad,
            up_bias_grad,
            down_weight_grad,
        ),
        "dp",
    )
    ln1_gain_grad, ln1_shift_grad, out_bias_grad, ln2_gain_grad, ln2_shift_grad, down_bias_grad = (
        lax.psum(
            (
                ln1_gain_grad,
                ln1_shift_grad,
                out_bias_grad,
                ln2_gain_grad,
                ln2_shift_grad,
                down_bias_grad,
            ),
            ("dp", "tensor"),
        )
    )
    return (
        output,
        input_grad,
        ln1_gain_grad,
        ln1_shift_grad,
        qkv_weight_grad,
        qkv_bias_grad,
        out_weight_grad,
        out_bias_grad,
        ln2_gain_grad,
        ln2_shift_grad,
        up_weight_grad,
        up_bias_grad,
        down_weight_grad,
        down_bias_grad,
    )


def solution(mesh):
    in_specs = (
        P("dp", "tensor", None),
        P("dp", "tensor", None),
        P("dp"),
        P(),
        P(),
        P(None, None, "tensor"),
        P(None, "tensor"),
        P("tensor", None),
        P(),
        P(),
        P(),
        P(None, "tensor"),
        P("tensor"),
        P("tensor", None),
        P(),
    )
    out_specs = (
        P("dp", "tensor", None),
        P("dp", "tensor", None),
        P(),
        P(),
        P(None, None, "tensor"),
        P(None, "tensor"),
        P("tensor", None),
        P(),
        P(),
        P(),
        P(None, "tensor"),
        P("tensor"),
        P("tensor", None),
        P(),
    )
    return jax.shard_map(body, mesh=mesh, in_specs=in_specs, out_specs=out_specs, check_vma=False)
```

profile of v0, /device:TPU:0, one launch (start us, length us, event | category | flops | bytes accessed | tf_op | source)
XLA Modules:
  0.0 1510.5 jit_solution(7519367030076174390)
XLA Ops:
  13.2 84.8 %all-gather.5.cloned.1.call-done = bf16[2,1024,2048]{2,1,0:T(8,128)(2,1)} async-done(((bf16[2,128,2048]{2,1,0:T(8,128)(2,1)}), bf16[2,1024,2048]{2,1,0:T(8,128)(2,1)}) %all-gather.5.cloned.1.call-update) | async-done | bytes 8388624 | tf_op jit(solution)/shard_map/all_gather | solution.py:129
  98.1 6.0 multiply_convert_fusion.3
  105.3 7.0 convolution_convert_fusion.3
  113.9 7.0 add_convert_fusion.3
  121.9 19.5 %while.26 = (s32[]{:T(128)}, bf16[2,1024,2,128]{1,3,2,0:T(8,128)(2,1)}, f32[2,2,1024,1]{2,1,3,0:T(2,128)S(1)}, bf16[2,1024,2,128]{1,3,2,0:T(8,128)(2,1)}, s32[2]...) while((s32[]{:T(128)}, ...), condition=%wide.region_7.8_spmd, body=%wide.region_2.7_spmd.sunk | while | flops 1093666304 | bytes 46220012 | solution.py:143
  141.4 7.4 convolution_convert_fusion.1
  148.9 88.2 %reduce-scatter.5.cloned.1.call-done = bf16[2,128,2048]{2,1,0:T(8,128)(2,1)} async-done(((bf16[2,1024,2048]{2,1,0:T(8,128)(2,1)}), bf16[2,128,2048]{2,1,0:T(8,128)(2,1)}) %reduce-scatter.5.cloned.1.call-update) | async-done | bytes 1048592 | tf_op jit(solution)/shard_map/reduce_scatter | solution.py:148
  245.1 77.9 %all-gather.7.cloned.1.call-done = bf16[2,1024,2048]{2,1,0:T(8,128)(2,1)} async-done(((bf16[2,128,2048]{2,1,0:T(8,128)(2,1)}), bf16[2,1024,2048]{2,1,0:T(8,128)(2,1)}) %all-gather.7.cloned.1.call-update) | async-done | bytes 8388624 | tf_op jit(solution)/shard_map/all_gather | solution.py:156
  323.0 15.6 %fusion.114 = (u8[1024,1024]{1,0:T(8,128)(4,1)S(1)}, u8[1024,1024]{1,0:T(8,128)(4,1)S(1)}, f32[2,1024,1024]{2,1,0:T(8,128)S(1)}) fusion(f32[1024]{0:T(1024)S(1)} %copy-done.47, bf16[2,1024,2048]{2,1,0:T(8,128)(2,1)} %all-gather.7.cloned.1.call-done, bf16[2048,1024]{1,0:T(8,128)(2,1)} %param.30), kind=kOutput, calls=%fused_computation.186 | convolution fusion | flops 8617197568 | bytes 23072768 | tf_op jit(solution)/shard_map/dot_general | solution.py:23
  342.0 20.5 %multiply_convert_fusion.2 = (bf16[2,1024,1024]{2,1,0:T(8,128)(2,1)}, f32[2,1024,1024]{2,1,0:T(8,128)}) fusion(f32[2,1024,1024]{2,1,0:T(8,128)S(1)} %get-tuple-element.211, f32[1024]{0:T(1024)S(1)} %copy-done.47, u8[1024,1024]{1,0:T(8,128)(4,1)S(1)} %get-tuple-element.129, u8[1024,1024]{1,0:T(8,128)(4,1)S(1)} %get-tuple-element.128), kind=kLoop, calls=%fused_computation.124 | loop fusion | flops 148897792 | bytes 23072768 | tf_op jit(solution)/shard_map/convert_element_type | solution.py:158
  362.6 43.1 %all-gather.9.cloned.1.call-done = bf16[2,1024,2048]{2,1,0:T(8,128)(2,1)} async-done(((bf16[2,128,2048]{2,1,0:T(8,128)(2,1)}), bf16[2,1024,2048]{2,1,0:T(8,128)(2,1)}) %all-gather.9.cloned.1.call-update) | async-done | bytes 8388624 | tf_op jit(solution)/shard_map/all_gather | solution.py:172
  405.6 21.2 %convert_reduce_fusion = (f32[1024]{0:T(1024)}, bf16[2,1024,1024]{2,1,0:T(8,128)(2,1)S(1)}) fusion(f32[2,1024,1024]{2,1,0:T(8,128)} %get-tuple-element.188, bf16[2,1024,2048]{2,1,0:T(8,128)(2,1)} %all-gather.9.cloned.1.call-done, bf16[1024,2048]{1,0:T(8,128)(2,1)} %param.32, f32[2,1024,1024]{2,1,0:T(8,128)} %copy-done.20, f32[1024]{0:T(1024)S(1)} %copy-done.47), kind=kOutput, calls=%fused_computation.122 | convolution fusion | flops 8625585152 | bytes 33562624 | tf_op jit(solution)/shard_map/dot_general | solution.py:29
  428.8 11.7 fusion.93
  440.6 14.3 convolution_convert_fusion
  455.0 152.5 %reduce-scatter.9.cloned.1.call-done = f32[2,128,2048]{2,1,0:T(8,128)} async-done(((f32[2,1024,2048]{2,1,0:T(8,128)}), f32[2,128,2048]{2,1,0:T(8,128)}) %reduce-scatter.9.cloned.1.call-update) | async-done | bytes 2097168 | tf_op jit(solution)/shard_map/reduce_scatter | solution.py:179
  611.0 87.2 %reduce-scatter.7.cloned.1.call-done = bf16[2,128,2048]{2,1,0:T(8,128)(2,1)} async-done(((bf16[2,1024,2048]{2,1,0:T(8,128)(2,1)}), bf16[2,128,2048]{2,1,0:T(8,128)(2,1)}) %reduce-scatter.7.cloned.1.call-update) | async-done | bytes 1048592 | tf_op jit(solution)/shard_map/reduce_scatter | solution.py:159
  698.2 4.3 fusion.139
  705.2 80.5 %all-gather.11.cloned.1.call-done = bf16[2,1024,2048]{2,1,0:T(8,128)(2,1)} async-done(((bf16[2,128,2048]{2,1,0:T(8,128)(2,1)}), bf16[2,1024,2048]{2,1,0:T(8,128)(2,1)}) %all-gather.11.cloned.1.call-update) | async-done | bytes 8388624 | tf_op jit(solution)/shard_map/all_gather | solution.py:186
  785.7 6.7 convolution_convert_fusion.2
  795.8 33.9 %while.27 = (s32[]{:T(128)}, bf16[2,1024,2,128]{1,3,2,0:T(8,128)(2,1)}, bf16[2,1024,2,128]{1,3,2,0:T(8,128)(2,1)}, bf16[2,1024,2,128]{1,3,2,0:T(8,128)(2,1)}, bf...) while((s32[]{:T(128)}, ...), condition=%wide.region_18.19_spmd, body=%wide.region_15.18_spmd.sunk | while | flops 2713189888 | bytes 113858456 | solution.py:189
  829.7 9.8 fusion.120
  839.4 9.5 fusion.117
  848.9 18.5 %add_add_fusion = f32[2,1024,2048]{2,1,0:T(8,128)} fusion(f32[2,1024,2048]{2,1,0:T(8,128)} %fusion.117, f32[2,1024,2048]{2,1,0:T(8,128)} %fusion.120, bf16[2,1024,256]{1,2,0:T(8,128)(2,1)S(1)} %bitcast.299, bf16[3,2048,256]{2,1,0:T(8,128)(2,1)} %param.24), kind=kOutput, calls=%fused_computation.114 | convolution fusion | flops 2160066560 | bytes 52428800 | tf_op jit(solution)/shard_map/dot_general | solution.py:29
  867.4 15.0 convolution_bitcast_fusion.3
  882.5 14.0 convolution_bitcast_fusion.2
  896.5 6.2 convolution_bitcast_fusion.5
  902.8 6.3 convolution_bitcast_fusion.6
  919.5 10.8 all-reduce.1
  930.3 104.0 %reduce-scatter.11.cloned.1.call-done = f32[2,128,2048]{2,1,0:T(8,128)} async-done(((f32[2,1024,2048]{2,1,0:T(8,128)}), f32[2,128,2048]{2,1,0:T(8,128)}) %reduce-scatter.11.cloned.1.call-update) | async-done | bytes 2097168 | tf_op jit(solution)/shard_map/reduce_scatter | solution.py:215
  1041.8 39.5 %all-reduce = (f32[2048]{0:T(1024)}, f32[2048]{0:T(1024)}, f32[2048]{0:T(1024)}, f32[2048]{0:T(1024)}, f32[2048]{0:T(1024)}, /*index=5*/f32[2048]{0:T(1024)}) all-reduce(f32[2048]{0:T(1024)S(1)} %get-tuple-element.132, f32[2048]{0:T(1024)S(1)} %get-tuple-element.135, ...), channel_id=1, replica_groups=mesh['dp'=4,'tensor'=8] {'dp','tensor'}, use_global_device_ids=true, to_apply=%region_23.24 | all-reduce | flops 12288 | bytes 98304 | tf_op jit(solution)/shard_map/psum | solution.py:238
  1081.3 404.6 %all-reduce.5.cloned.1.call-done = (f32[3,2048,256]{2,1,0:T(8,128)}, f32[256,2048]{1,0:T(8,128)}, f32[2048,1024]{1,0:T(8,128)}, f32[1024,2048]{1,0:T(8,128)}) async-done(((f32[3,2048,256]{2,1,0:T(8,128)}, f32[256,2048]{1,0:T(8,128)}, f32[2048,1024]{1,0:T(8,128)}, f32[1024,2048]{1,0:T(8,128)}), (f32[3,2048,256]{2,1,0:T(8,128)}, f32[256,2048]{1,0:T(8,128)}, f32[2048,1024]{1,0:T(8,128)}, ...) | async-done | bytes 25165840 | tf_op jit(solution)/shard_map/psum | solution.py:226
  1486.0 6.6 copy.120
  (262 shorter events, 114.1 us)
Async XLA Ops:
  7.2 134.2 %copy-start = (bf16[256,2048]{1,0:T(8,128)(2,1)S(1)}, bf16[256,2048]{1,0:T(8,128)(2,1)}, u32[]{:S(2)}) copy-start(bf16[256,2048]{1,0:T(8,128)(2,1)} %param.26) | copy-start | bytes 3145732
  7.2 90.9 %all-gather.5.cloned.1.call-start = ((), (), s32[]{:S(2)}) async-start(), calls=%async_computation.4 | async-start | bytes 9437184 | tf_op jit(solution)/shard_map/all_gather | solution.py:129
  8.8 89.3 %copy-start.33 = (f32[2,128]{1,0:T(2,128)}, f32[2,128]{1,0:T(2,128)S(1)}, u32[]{:S(2)}) copy-start(f32[2,128]{1,0:T(2,128)S(1)} %broadcast_multiply_fusion.2) | copy-start | bytes 3076
  10.4 87.6 %copy-start.41 = (f32[2,128]{1,0:T(2,128)}, f32[2,128]{1,0:T(2,128)S(1)}, u32[]{:S(2)}) copy-start(f32[2,128]{1,0:T(2,128)S(1)} %fusion.108) | copy-start | bytes 3076
  10.5 87.6 %copy-start.37 = (f32[2,128]{1,0:T(2,128)}, f32[2,128]{1,0:T(2,128)S(1)}, u32[]{:S(2)}) copy-start(f32[2,128]{1,0:T(2,128)S(1)} %fusion.136) | copy-start | bytes 3076
  13.2 224.0 %reduce-scatter.5.cloned.1.call-start = ((), (), s32[]{:S(2)}) async-start(), calls=%async_computation.5 | async-start | bytes 9437184 | tf_op jit(solution)/shard_map/reduce_scatter | solution.py:148
  148.8 88.3 %copy-start.2 = (bf16[2,128,2048]{2,1,0:T(8,128)(2,1)S(1)}, bf16[2,128,2048]{2,1,0:T(8,128)(2,1)}, u32[]{:S(2)}) copy-start(bf16[2,128,2048]{2,1,0:T(8,128)(2,1)} %param.19) | copy-start | bytes 3145732
  148.8 88.3 %copy-start.30 = (f32[2048]{0:T(1024)S(1)}, f32[2048]{0:T(1024)}, u32[]{:S(2)}) copy-start(f32[2048]{0:T(1024)} %param.27) | copy-start | bytes 24580
  148.8 91.9 %copy-start.32 = (f32[2048]{0:T(1024)S(1)}, f32[2048]{0:T(1024)}, u32[]{:S(2)}) copy-start(f32[2048]{0:T(1024)} %param.28) | copy-start | bytes 24580
  148.9 91.9 %copy-start.45 = (f32[2048]{0:T(1024)S(1)}, f32[2048]{0:T(1024)}, u32[]{:S(2)}) copy-start(f32[2048]{0:T(1024)} %param.29) | copy-start | bytes 24580
  148.9 174.1 %all-gather.7.cloned.1.call-start = ((), (), s32[]{:S(2)}) async-start(), calls=%async_computation.6 | async-start | bytes 9437184 | tf_op jit(solution)/shard_map/all_gather | solution.py:156
  240.7 82.3 %copy-start.47 = (f32[1024]{0:T(1024)S(1)}, f32[1024]{0:T(1024)}, u32[]{:S(2)}) copy-start(f32[1024]{0:T(1024)} %param.31) | copy-start | bytes 12292
  242.4 163.2 %all-gather.9.cloned.1.call-start = ((), (), s32[]{:S(2)}) async-start(), calls=%async_computation.8 | async-start | bytes 9437184 | tf_op jit(solution)/shard_map/all_gather | solution.py:172
  242.6 460.0 %copy-start.39 = (f32[2,128]{1,0:T(2,128)}, f32[2,128]{1,0:T(2,128)S(1)}, u32[]{:S(2)}) copy-start(f32[2,128]{1,0:T(2,128)S(1)} %compare_convert_fusion) | copy-start | bytes 3076
  245.0 362.5 %reduce-scatter.9.cloned.1.call-start = ((), (), s32[]{:S(2)}) async-start(), calls=%async_computation.9 | async-start | bytes 18874368 | tf_op jit(solution)/shard_map/reduce_scatter | solution.py:179
  405.6 23.2 %copy-start.51 = (bf16[2048,1024]{1,0:T(8,128)(2,1)S(1)}, bf16[2048,1024]{1,0:T(8,128)(2,1)}, u32[]{:S(2)}) copy-start(bf16[2048,1024]{1,0:T(8,128)(2,1)} %param.30) | copy-start | bytes 12582916
  440.6 257.7 %reduce-scatter.7.cloned.1.call-start = ((), (), s32[]{:S(2)}) async-start(), calls=%async_computation.7 | async-start | bytes 9437184 | tf_op jit(solution)/shard_map/reduce_scatter | solution.py:159
  455.0 243.3 %copy-start.46 = (f32[2048]{0:T(1024)S(1)}, f32[2048]{0:T(1024)}, u32[]{:S(2)}) copy-start(f32[2048]{0:T(1024)} %param.33) | copy-start | bytes 24580
  455.0 330.8 %all-gather.11.cloned.1.call-start = ((), (), s32[]{:S(2)}) async-start(), calls=%async_computation.10 | async-start | bytes 9437184 | tf_op jit(solution)/shard_map/all_gather | solution.py:186
  702.5 90.0 %copy-start.43 = (f32[2,128]{1,0:T(2,128)}, f32[2,128]{1,0:T(2,128)S(1)}, u32[]{:S(2)}) copy-start(f32[2,128]{1,0:T(2,128)S(1)} %negate_multiply_fusion.2) | copy-start | bytes 3076
  705.2 329.1 %reduce-scatter.11.cloned.1.call-start = ((), (), s32[]{:S(2)}) async-start(), calls=%async_computation.11 | async-start | bytes 18874368 | tf_op jit(solution)/shard_map/reduce_scatter | solution.py:215
  705.2 90.5 %copy-start.5 = (bf16[2,1024,2,128]{3,1,2,0:T(8,128)(2,1)S(1)}, bf16[2,1024,2,128]{3,1,2,0:T(8,128)(2,1)}, u32[]{:S(2)}) copy-start(bf16[2,1024,2,128]{3,1,2,0:T(8,128)(2,1)} %copy-done.4) | copy-start | bytes 3145732
  867.4 618.6 %all-reduce.5.cloned.1.call-start = ((), (), s32[]{:S(2)}) async-start(), calls=%async_computation.12 | async-start | bytes 50331648 | tf_op jit(solution)/shard_map/psum | solution.py:226
  867.4 15.0 copy-start.28
  918.8 115.5 %copy-start.3 = (bf16[2,128,2048]{2,1,0:T(8,128)(2,1)S(1)}, bf16[2,128,2048]{2,1,0:T(8,128)(2,1)}, u32[]{:S(2)}) copy-start(bf16[2,128,2048]{2,1,0:T(8,128)(2,1)} %param.19) | copy-start | bytes 3145732
  918.8 115.5 %copy-start.31 = (f32[2048]{0:T(1024)S(1)}, f32[2048]{0:T(1024)}, u32[]{:S(2)}) copy-start(f32[2048]{0:T(1024)} %param.22) | copy-start | bytes 24580
  918.8 115.6 %copy-start.34 = (f32[2,128]{1,0:T(2,128)S(1)}, f32[2,128]{1,0:T(2,128)}, u32[]{:S(2)}) copy-start(f32[2,128]{1,0:T(2,128)} %copy-done.33) | copy-start | bytes 3076
  918.8 117.8 %copy-start.42 = (f32[2,128]{1,0:T(2,128)S(1)}, f32[2,128]{1,0:T(2,128)}, u32[]{:S(2)}) copy-start(f32[2,128]{1,0:T(2,128)} %copy-done.41) | copy-start | bytes 3076
  918.8 117.8 %copy-start.38 = (f32[2,128]{1,0:T(2,128)S(1)}, f32[2,128]{1,0:T(2,128)}, u32[]{:S(2)}) copy-start(f32[2,128]{1,0:T(2,128)} %copy-done.37) | copy-start | bytes 3076
  918.8 118.7 %copy-start.40 = (f32[2,128]{1,0:T(2,128)S(1)}, f32[2,128]{1,0:T(2,128)}, u32[]{:S(2)}) copy-start(f32[2,128]{1,0:T(2,128)} %copy-done.39) | copy-start | bytes 3076
  918.8 118.7 %copy-start.44 = (f32[2,128]{1,0:T(2,128)S(1)}, f32[2,128]{1,0:T(2,128)}, u32[]{:S(2)}) copy-start(f32[2,128]{1,0:T(2,128)} %copy-done.43) | copy-start | bytes 3076
  919.2 118.4 %copy-start.19 = (bf16[2,128,2048]{2,1,0:T(8,128)(2,1)S(1)}, bf16[2,128,2048]{2,1,0:T(8,128)(2,1)}, u32[]{:S(2)}) copy-start(bf16[2,128,2048]{2,1,0:T(8,128)(2,1)} %param.20) | copy-start | bytes 3145732
  (47 other events, 177.2 us)
Sparse Core Ops, SparseCore 0:
  13.3 84.7 all-gather.4
  149.0 88.1 reduce-scatter.4
  242.5 80.3 all-gather.6
  325.0 80.5 all-gather.8
  440.7 166.7 reduce-scatter.8
  610.2 87.9 reduce-scatter.6
  705.3 80.3 all-gather.10
  867.5 166.7 reduce-scatter.10
  1039.4 446.4 all-reduce.4
where the time goes:
time: 1510 us
  waiting for transfers between devices  1120 us (74%)
  matrix products  212 us (14%)
  other arithmetic  68.2 us (5%)
  blocking collectives  50.4 us (3%)
  local copies, waits for them, and re-layouts  40.8 us (3%)
    psum x1, waiting for transfers between devices, body(): lax.psum((qkv_weight_grad, qkv_bias_grad, out_weight_grad, up_weight_grad...  405 us
    reduce_scatter x1, waiting for transfers between devices, body(): lax.psum_scatter(product_back(grad_pre, up_weight), 'tensor', scatter_dim...  152 us
    reduce_scatter x1, waiting for transfers between devices, body(): lax.psum_scatter(norm_one_part, 'tensor', scatter_dimension=1, tiled=True)  104 us
    reduce_scatter x1, waiting for transfers between devices, body(): lax.psum_scatter(flat_product(mixed_heads, out_weight).astype(jnp.bfloat1...  88.2 us
    reduce_scatter x1, waiting for transfers between devices, body(): lax.psum_scatter(flat_product(activated, down_weight).astype(jnp.bfloat16...  87.2 us
    all_gather x1, waiting for transfers between devices, body(): gathered_one = lax.all_gather(normed_one, 'tensor', axis=1, tiled=True)  84.8 us
    all_gather x1, waiting for transfers between devices, body(): lax.all_gather(hidden_grad.astype(jnp.bfloat16), 'tensor', axis=1, tiled=...  80.5 us
    all_gather x1, waiting for transfers between devices, body(): gathered_two = lax.all_gather(normed_two, 'tensor', axis=1, tiled=True)  77.9 us
  transfers between devices with their start and end apart: 9, of which 9 were waited for; matrix products, arithmetic and copies ran while one was open for 8% of the time, Pallas kernels for 0%

commit v1 on v0

--- a/solution.py
+++ b/solution.py
@@ -1,3 +1,4 @@
+import functools
 import jax
 import jax.numpy as jnp
 from jax import lax
@@ -6,6 +7,32 @@
 HD = 128
 norm_epsilon = 1e-05
 block_rows = 512
+
+
+def _remake_steps_all(my_tile, ndim_at):
+    w_next = list(my_tile.shape[1:])
+    w_next[ndim_at] *= my_tile.shape[0]
+    return jnp.moveaxis(my_tile, 0, ndim_at).reshape(w_next)
+
+
+def _mark_outputs(my_data, across):
+    world = lax.psum(1, across)
+    work_now = my_data[None]
+    for tick in range(world.bit_length() - 1):
+        top = 1 << tick
+        outer = lax.ppermute(work_now, across, [(q, q ^ top) for q in range(world)])
+        z1 = jnp.stack([work_now, outer], axis=0)
+        oldest = lax.axis_index(across) >> tick & 1
+        work_now = jnp.where(oldest == 0, z1, z1[::-1]).reshape(-1, *my_data.shape)
+    return work_now
+
+
+def play_the_panels(x0, point, in_dim):
+    res = _mark_outputs(x0, point)
+    return _remake_steps_all(res, in_dim)
+
+
+carry_case_up = functools.partial(play_the_panels, point="tensor", in_dim=1)
 
 
 def layer_norm(values, norm_gain, norm_shift):
@@ -169,7 +196,7 @@
     valid_rows = (slot_ids < lengths[:, None]).astype(jnp.float32)
     grad_out = cotangent.astype(jnp.float32) * valid_rows[:, :, None]
     down_bias_grad = jnp.sum(grad_out, axis=(0, 1))
-    grad_mlp = lax.all_gather(grad_out.astype(jnp.bfloat16), "tensor", axis=1, tiled=True)
+    grad_mlp = carry_case_up(grad_out.astype(jnp.bfloat16))
     down_weight_grad = rows_product(activated, grad_mlp)
     grad_act = product_back(grad_mlp, down_weight)
     unused_act, gelu_back = jax.vjp(gelu_exact, pre_act)

time: 1510 us -> 1730 us (1.15)
  waiting for transfers between devices: 1120 us -> 1300 us
  other arithmetic: 68.2 us -> 101 us
    ppermute x0 -> x3, waiting for transfers between devices: none -> 297 us  [_mark_outputs(): outer = lax.ppermute(work_now, across, [(q, q ^ top) for q in range(world)])]
    all_gather x1, waiting for transfers between devices: 77.9 us -> 0.01 us  [body(): gathered_two = lax.all_gather(normed_two, 'tensor', axis=1, tiled=True)]
    all_gather x1 -> x0, waiting for transfers between devices: 43.1 us -> none  [body(): lax.all_gather(grad_out.astype(jnp.bfloat16), 'tensor', axis=1, tiled=True)]
    another operation x0 -> x5, other arithmetic: none -> 17.7 us  [_mark_outputs(): z1 = jnp.stack([work_now, outer], axis=0)]
    select_n x0 -> x2, other arithmetic: none -> 17.5 us  [_mark_outputs(): work_now = jnp.where(oldest == 0, z1, z1[::-1]).reshape(-1, *my_data.shape)]
  transfers between devices with their start and end apart: 9 -> 11, of which waited for: 9 -> 10; matrix products, arithmetic and copies ran while one was open for 8% -> 7% of each run, Pallas kernels for 0% -> 0%
where the time goes in v1:
time: 1730 us
  waiting for transfers between devices  1300 us (75%)
  matrix products  214 us (12%)
  other arithmetic  101 us (6%)
  blocking collectives  50.5 us (3%)
  local copies, waits for them, and re-layouts  43.2 us (2%)
    psum x1, waiting for transfers between devices, body(): lax.psum((qkv_weight_grad, qkv_bias_grad, out_weight_grad, up_weight_grad...  405 us
    ppermute x3, waiting for transfers between devices, _mark_outputs(): outer = lax.ppermute(work_now, across, [(q, q ^ top) for q in range(world)])  297 us
    reduce_scatter x1, waiting for transfers between devices, body(): lax.psum_scatter(product_back(grad_pre, up_weight), 'tensor', scatter_dim...  153 us
    reduce_scatter x1, waiting for transfers between devices, body(): lax.psum_scatter(norm_one_part, 'tensor', scatter_dimension=1, tiled=True)  104 us
    reduce_scatter x1, waiting for transfers between devices, body(): lax.psum_scatter(flat_product(mixed_heads, out_weight).astype(jnp.bfloat1...  88.2 us
    reduce_scatter x1, waiting for transfers between devices, body(): lax.psum_scatter(flat_product(activated, down_weight).astype(jnp.bfloat16...  87.2 us
    all_gather x1, waiting for transfers between devices, body(): gathered_one = lax.all_gather(normed_one, 'tensor', axis=1, tiled=True)  84.8 us
    all_gather x1, waiting for transfers between devices, body(): lax.all_gather(hidden_grad.astype(jnp.bfloat16), 'tensor', axis=1, tiled=...  80.5 us
  transfers between devices with their start and end apart: 11, of which 10 were waited for; matrix products, arithmetic and copies ran while one was open for 7% of the time, Pallas kernels for 0%

profile of v1, /device:TPU:0, one launch (start us, length us, event | category | flops | bytes accessed | tf_op | source)
XLA Modules:
  0.0 1725.7 jit_solution(18233081474607756860)
XLA Ops:
  13.2 84.8 %all-gather.4.cloned.1.call-done = bf16[2,1024,2048]{2,1,0:T(8,128)(2,1)} async-done(((bf16[2,128,2048]{2,1,0:T(8,128)(2,1)}), bf16[2,1024,2048]{2,1,0:T(8,128)(2,1)}) %all-gather.4.cloned.1.call-update) | async-done | bytes 8388624 | tf_op jit(solution)/shard_map/all_gather | solution.py:156
  104.9 7.0 convolution_convert_fusion.3
  113.5 7.0 add_convert_fusion.3
  121.6 19.5 %while.26 = (s32[]{:T(128)}, bf16[2,1024,2,128]{1,3,2,0:T(8,128)(2,1)}, f32[2,2,1024,1]{2,1,3,0:T(2,128)S(1)}, bf16[2,1024,2,128]{1,3,2,0:T(8,128)(2,1)}, s32[2]...) while((s32[]{:T(128)}, ...), condition=%wide.region_7.8_spmd, body=%wide.region_2.7_spmd.sunk | while | flops 1093666304 | bytes 46220012 | solution.py:170
  141.1 7.4 convolution_convert_fusion.1
  148.6 88.2 %reduce-scatter.5.cloned.1.call-done = bf16[2,128,2048]{2,1,0:T(8,128)(2,1)} async-done(((bf16[2,1024,2048]{2,1,0:T(8,128)(2,1)}), bf16[2,128,2048]{2,1,0:T(8,128)(2,1)}) %reduce-scatter.5.cloned.1.call-update) | async-done | bytes 1048592 | tf_op jit(solution)/shard_map/reduce_scatter | solution.py:175
  252.7 111.3 %collective-permute-done.1 = bf16[2,2,128,2048]{3,2,1,0:T(8,128)(2,1)} collective-permute-done((bf16[2,2,128,2048]{3,2,1,0:T(8,128)(2,1)}, bf16[2,2,128,2048]{3,2,1,0:T(8,128)(2,1)}, u32[]{:S(2)}, u32[]{:S(2)}) %collective-permute-start.1) | collective-permute-done | bytes 2097184 | tf_op jit(solution)/shard_map/ppermute | solution.py:23
  370.3 182.8 %collective-permute-done.2 = bf16[4,2,128,2048]{3,2,1,0:T(8,128)(2,1)} collective-permute-done((bf16[4,2,128,2048]{3,2,1,0:T(8,128)(2,1)}, bf16[4,2,128,2048]{3,2,1,0:T(8,128)(2,1)}, u32[]{:S(2)}, u32[]{:S(2)}) %collective-permute-start.2) | collective-permute-done | bytes 4194336 | tf_op jit(solution)/shard_map/ppermute | solution.py:23
  553.1 7.6 pad_maximum_fusion
  560.7 14.3 reverse_select_fusion
  575.0 8.3 copy.41
  583.3 15.9 fusion.114
  599.2 20.6 %multiply_convert_fusion.2 = (bf16[2,1024,1024]{2,1,0:T(8,128)(2,1)}, f32[2,1024,1024]{2,1,0:T(8,128)}) fusion(f32[2,1024,1024]{2,1,0:T(8,128)S(1)} %get-tuple-element.215, f32[1024]{0:T(1024)S(1)} %copy-done.46, u8[1024,1024]{1,0:T(8,128)(4,1)S(1)} %get-tuple-element.129, u8[1024,1024]{1,0:T(8,128)(4,1)S(1)} %get-tuple-element.128), kind=kLoop, calls=%fused_computation.126 | loop fusion | flops 148897792 | bytes 23072768 | tf_op jit(solution)/shard_map/convert_element_type | solution.py:185
  619.7 19.8 %convert_reduce_fusion = (f32[1024]{0:T(1024)}, bf16[2,1024,1024]{2,1,0:T(8,128)(2,1)}) fusion(f32[2,1024,1024]{2,1,0:T(8,128)} %get-tuple-element.188, bf16[2,1024,2048]{2,1,0:T(8,128)(2,1)} %bitcast.322, bf16[1024,2048]{1,0:T(8,128)(2,1)} %param.32, f32[2,1024,1024]{2,1,0:T(8,128)S(1)} %get-tuple-element.215, f32[1024]{0:T(1024)S(1)} %copy-done.46), kind=kOutput, calls=%fused_computation.124 | convolution fusion | flops 8625585152 | bytes 33562624 | tf_op jit(solution)/shard_map/dot_general | solution.py:56
  639.6 15.3 fusion.93
  655.0 14.1 convolution_convert_fusion
  669.2 153.3 %reduce-scatter.9.cloned.1.call-done = f32[2,128,2048]{2,1,0:T(8,128)} async-done(((f32[2,1024,2048]{2,1,0:T(8,128)}), f32[2,128,2048]{2,1,0:T(8,128)}) %reduce-scatter.9.cloned.1.call-update) | async-done | bytes 2097168 | tf_op jit(solution)/shard_map/reduce_scatter | solution.py:206
  826.0 87.2 %reduce-scatter.7.cloned.1.call-done = bf16[2,128,2048]{2,1,0:T(8,128)(2,1)} async-done(((bf16[2,1024,2048]{2,1,0:T(8,128)(2,1)}), bf16[2,128,2048]{2,1,0:T(8,128)(2,1)}) %reduce-scatter.7.cloned.1.call-update) | async-done | bytes 1048592 | tf_op jit(solution)/shard_map/reduce_scatter | solution.py:186
  920.2 80.5 %all-gather.8.cloned.1.call-done = bf16[2,1024,2048]{2,1,0:T(8,128)(2,1)} async-done(((bf16[2,128,2048]{2,1,0:T(8,128)(2,1)}), bf16[2,1024,2048]{2,1,0:T(8,128)(2,1)}) %all-gather.8.cloned.1.call-update) | async-done | bytes 8388624 | tf_op jit(solution)/shard_map/all_gather | solution.py:213
  1000.7 6.7 convolution_convert_fusion.2
  1010.7 33.6 %while.27 = (s32[]{:T(128)}, bf16[2,1024,2,128]{1,3,2,0:T(8,128)(2,1)}, bf16[2,1024,2,128]{1,3,2,0:T(8,128)(2,1)}, bf16[2,1024,2,128]{1,3,2,0:T(8,128)(2,1)}, bf...) while((s32[]{:T(128)}, ...), condition=%wide.region_18.19_spmd, body=%wide.region_15.18_spmd.sunk | while | flops 2713189888 | bytes 113858456 | solution.py:216
  1044.3 9.8 fusion.122
  1054.1 9.5 fusion.119
  1063.6 18.5 %add_add_fusion = f32[2,1024,2048]{2,1,0:T(8,128)} fusion(f32[2,1024,2048]{2,1,0:T(8,128)} %fusion.119, f32[2,1024,2048]{2,1,0:T(8,128)} %fusion.122, bf16[2,1024,256]{1,2,0:T(8,128)(2,1)S(1)} %bitcast.318, bf16[3,2048,256]{2,1,0:T(8,128)(2,1)} %param.24), kind=kOutput, calls=%fused_computation.114 | convolution fusion | flops 2160066560 | bytes 52428800 | tf_op jit(solution)/shard_map/dot_general | solution.py:56
  1082.1 15.0 convolution_bitcast_fusion.2
  1097.1 13.8 fusion.146
  1117.3 6.3 convolution_bitcast_fusion.5
  1133.9 11.0 all-reduce.1
  1144.9 104.2 %reduce-scatter.11.cloned.1.call-done = f32[2,128,2048]{2,1,0:T(8,128)} async-done(((f32[2,1024,2048]{2,1,0:T(8,128)}), f32[2,128,2048]{2,1,0:T(8,128)}) %reduce-scatter.11.cloned.1.call-update) | async-done | bytes 2097168 | tf_op jit(solution)/shard_map/reduce_scatter | solution.py:242
  1256.5 39.5 %all-reduce = (f32[2048]{0:T(1024)}, f32[2048]{0:T(1024)}, f32[2048]{0:T(1024)}, f32[2048]{0:T(1024)}, f32[2048]{0:T(1024)}, /*index=5*/f32[2048]{0:T(1024)}) all-reduce(f32[2048]{0:T(1024)S(1)} %get-tuple-element.132, f32[2048]{0:T(1024)S(1)} %get-tuple-element.135, ...), channel_id=1, replica_groups=mesh['dp'=4,'tensor'=8] {'dp','tensor'}, use_global_device_ids=true, to_apply=%region_23.24 | all-reduce | flops 12288 | bytes 98304 | tf_op jit(solution)/shard_map/psum | solution.py:265
  1296.0 404.6 %all-reduce.5.cloned.1.call-done = (f32[3,2048,256]{2,1,0:T(8,128)}, f32[256,2048]{1,0:T(8,128)}, f32[2048,1024]{1,0:T(8,128)}, f32[1024,2048]{1,0:T(8,128)}) async-done(((f32[3,2048,256]{2,1,0:T(8,128)}, f32[256,2048]{1,0:T(8,128)}, f32[2048,1024]{1,0:T(8,128)}, f32[1024,2048]{1,0:T(8,128)}), (f32[3,2048,256]{2,1,0:T(8,128)}, f32[256,2048]{1,0:T(8,128)}, f32[2048,1024]{1,0:T(8,128)}, ...) | async-done | bytes 25165840 | tf_op jit(solution)/shard_map/psum | solution.py:253
  1700.7 6.6 copy.119
  (266 shorter events, 138.6 us)
Async XLA Ops:
  7.2 133.9 %copy-start = (bf16[256,2048]{1,0:T(8,128)(2,1)S(1)}, bf16[256,2048]{1,0:T(8,128)(2,1)}, u32[]{:S(2)}) copy-start(bf16[256,2048]{1,0:T(8,128)(2,1)} %param.26) | copy-start | bytes 3145732
  7.2 90.9 %all-gather.4.cloned.1.call-start = ((), (), s32[]{:S(2)}) async-start(), calls=%async_computation.4 | async-start | bytes 9437184 | tf_op jit(solution)/shard_map/all_gather | solution.py:156
  8.8 89.3 %copy-start.32 = (f32[2,128]{1,0:T(2,128)}, f32[2,128]{1,0:T(2,128)S(1)}, u32[]{:S(2)}) copy-start(f32[2,128]{1,0:T(2,128)S(1)} %broadcast_multiply_fusion.2) | copy-start | bytes 3076
  10.4 87.6 %copy-start.40 = (f32[2,128]{1,0:T(2,128)}, f32[2,128]{1,0:T(2,128)S(1)}, u32[]{:S(2)}) copy-start(f32[2,128]{1,0:T(2,128)S(1)} %fusion.108) | copy-start | bytes 3076
  10.5 87.6 %copy-start.36 = (f32[2,128]{1,0:T(2,128)}, f32[2,128]{1,0:T(2,128)S(1)}, u32[]{:S(2)}) copy-start(f32[2,128]{1,0:T(2,128)S(1)} %fusion.140) | copy-start | bytes 3076
  13.2 223.7 %reduce-scatter.5.cloned.1.call-start = ((), (), s32[]{:S(2)}) async-start(), calls=%async_computation.5 | async-start | bytes 9437184 | tf_op jit(solution)/shard_map/reduce_scatter | solution.py:175
  148.5 88.3 %copy-start.2 = (bf16[2,128,2048]{2,1,0:T(8,128)(2,1)S(1)}, bf16[2,128,2048]{2,1,0:T(8,128)(2,1)}, u32[]{:S(2)}) copy-start(bf16[2,128,2048]{2,1,0:T(8,128)(2,1)} %param.19) | copy-start | bytes 3145732
  148.5 88.3 %copy-start.29 = (f32[2048]{0:T(1024)S(1)}, f32[2048]{0:T(1024)}, u32[]{:S(2)}) copy-start(f32[2048]{0:T(1024)} %param.27) | copy-start | bytes 24580
  148.5 91.9 %copy-start.31 = (f32[2048]{0:T(1024)S(1)}, f32[2048]{0:T(1024)}, u32[]{:S(2)}) copy-start(f32[2048]{0:T(1024)} %param.28) | copy-start | bytes 24580
  148.6 91.8 %copy-start.44 = (f32[2048]{0:T(1024)S(1)}, f32[2048]{0:T(1024)}, u32[]{:S(2)}) copy-start(f32[2048]{0:T(1024)} %param.29) | copy-start | bytes 24580
  148.6 434.7 %all-gather.6.cloned.1.call-start = ((), (), s32[]{:S(2)}) async-start(), calls=%async_computation.6 | async-start | bytes 9437184 | tf_op jit(solution)/shard_map/all_gather | solution.py:183
  242.1 580.4 %reduce-scatter.9.cloned.1.call-start = ((), (), s32[]{:S(2)}) async-start(), calls=%async_computation.8 | async-start | bytes 18874368 | tf_op jit(solution)/shard_map/reduce_scatter | solution.py:206
  242.2 675.2 %copy-start.38 = (f32[2,128]{1,0:T(2,128)}, f32[2,128]{1,0:T(2,128)S(1)}, u32[]{:S(2)}) copy-start(f32[2,128]{1,0:T(2,128)S(1)} %compare_convert_fusion) | copy-start | bytes 3076
  245.0 3.0 collective-permute-start
  252.7 111.3 %collective-permute-start.1 = (bf16[2,2,128,2048]{3,2,1,0:T(8,128)(2,1)}, bf16[2,2,128,2048]{3,2,1,0:T(8,128)(2,1)}, u32[]{:S(2)}, u32[]{:S(2)}) collective-permute-start(bf16[2,2,128,2048]{3,2,1,0:T(8,128)(2,1)} %get-tuple-element.210), channel_id=1, source_target_pairs={{0,2},{1,3},{2,0},{3,1},{4,6},{5,7},{6,4},{7,5},{8,10},{9,11},{10,... | collective-permute-start | bytes 6291464 | tf_op jit(solution)/shard_map/ppermute | solution.py:23
  369.8 183.3 %collective-permute-start.2 = (bf16[4,2,128,2048]{3,2,1,0:T(8,128)(2,1)}, bf16[4,2,128,2048]{3,2,1,0:T(8,128)(2,1)}, u32[]{:S(2)}, u32[]{:S(2)}) collective-permute-start(bf16[4,2,128,2048]{3,2,1,0:T(8,128)(2,1)} %bitcast.50), channel_id=1, source_target_pairs={{0,4},{1,5},{2,6},{3,7},{4,0},{5,1},{6,2},{7,3},{8,12},{9,13},{10,... | collective-permute-start | bytes 12582920 | tf_op jit(solution)/shard_map/ppermute | solution.py:23
  654.9 258.3 %reduce-scatter.7.cloned.1.call-start = ((), (), s32[]{:S(2)}) async-start(), calls=%async_computation.7 | async-start | bytes 9437184 | tf_op jit(solution)/shard_map/reduce_scatter | solution.py:186
  669.1 244.0 %copy-start.45 = (f32[2048]{0:T(1024)S(1)}, f32[2048]{0:T(1024)}, u32[]{:S(2)}) copy-start(f32[2048]{0:T(1024)} %param.33) | copy-start | bytes 24580
  669.1 331.5 %all-gather.8.cloned.1.call-start = ((), (), s32[]{:S(2)}) async-start(), calls=%async_computation.9 | async-start | bytes 9437184 | tf_op jit(solution)/shard_map/all_gather | solution.py:213
  917.4 90.0 %copy-start.42 = (f32[2,128]{1,0:T(2,128)}, f32[2,128]{1,0:T(2,128)S(1)}, u32[]{:S(2)}) copy-start(f32[2,128]{1,0:T(2,128)S(1)} %negate_multiply_fusion.2) | copy-start | bytes 3076
  920.1 328.9 %reduce-scatter.11.cloned.1.call-start = ((), (), s32[]{:S(2)}) async-start(), calls=%async_computation.10 | async-start | bytes 18874368 | tf_op jit(solution)/shard_map/reduce_scatter | solution.py:242
  920.2 90.6 %copy-start.5 = (bf16[2,1024,2,128]{3,1,2,0:T(8,128)(2,1)S(1)}, bf16[2,1024,2,128]{3,1,2,0:T(8,128)(2,1)}, u32[]{:S(2)}) copy-start(bf16[2,1024,2,128]{3,1,2,0:T(8,128)(2,1)} %copy-done.4) | copy-start | bytes 3145732
  1082.1 618.6 %all-reduce.5.cloned.1.call-start = ((), (), s32[]{:S(2)}) async-start(), calls=%async_computation.11 | async-start | bytes 50331648 | tf_op jit(solution)/shard_map/psum | solution.py:253
  1082.1 15.0 copy-start.27
  1133.2 115.8 %copy-start.3 = (bf16[2,128,2048]{2,1,0:T(8,128)(2,1)S(1)}, bf16[2,128,2048]{2,1,0:T(8,128)(2,1)}, u32[]{:S(2)}) copy-start(bf16[2,128,2048]{2,1,0:T(8,128)(2,1)} %param.19) | copy-start | bytes 3145732
  1133.2 115.8 %copy-start.30 = (f32[2048]{0:T(1024)S(1)}, f32[2048]{0:T(1024)}, u32[]{:S(2)}) copy-start(f32[2048]{0:T(1024)} %param.22) | copy-start | bytes 24580
  1133.2 115.8 %copy-start.33 = (f32[2,128]{1,0:T(2,128)S(1)}, f32[2,128]{1,0:T(2,128)}, u32[]{:S(2)}) copy-start(f32[2,128]{1,0:T(2,128)} %copy-done.32) | copy-start | bytes 3076
  1133.3 118.1 %copy-start.41 = (f32[2,128]{1,0:T(2,128)S(1)}, f32[2,128]{1,0:T(2,128)}, u32[]{:S(2)}) copy-start(f32[2,128]{1,0:T(2,128)} %copy-done.40) | copy-start | bytes 3076
  1133.3 118.1 %copy-start.37 = (f32[2,128]{1,0:T(2,128)S(1)}, f32[2,128]{1,0:T(2,128)}, u32[]{:S(2)}) copy-start(f32[2,128]{1,0:T(2,128)} %copy-done.36) | copy-start | bytes 3076
  1133.3 119.0 %copy-start.39 = (f32[2,128]{1,0:T(2,128)S(1)}, f32[2,128]{1,0:T(2,128)}, u32[]{:S(2)}) copy-start(f32[2,128]{1,0:T(2,128)} %copy-done.38) | copy-start | bytes 3076
  1133.3 119.0 %copy-start.43 = (f32[2,128]{1,0:T(2,128)S(1)}, f32[2,128]{1,0:T(2,128)}, u32[]{:S(2)}) copy-start(f32[2,128]{1,0:T(2,128)} %copy-done.42) | copy-start | bytes 3076
  1133.7 118.6 %copy-start.19 = (bf16[2,128,2048]{2,1,0:T(8,128)(2,1)S(1)}, bf16[2,128,2048]{2,1,0:T(8,128)(2,1)}, u32[]{:S(2)}) copy-start(bf16[2,128,2048]{2,1,0:T(8,128)(2,1)} %param.20) | copy-start | bytes 3145732
  (46 other events, 180.1 us)
Sparse Core Ops, SparseCore 0:
  13.3 84.7 all-gather.3
  148.7 88.1 reduce-scatter.4
  242.2 119.6 all-gather.5
  655.0 167.3 reduce-scatter.8
  825.2 87.9 reduce-scatter.6
  920.2 80.4 all-gather.7
  1082.2 166.7 reduce-scatter.10
  1254.1 446.5 all-reduce.4
